TPU v7x, 512 devices: a whole 4x4x16 slice. The times are simulated.
512 devices in a mesh: tm: 32 (over y, z_lo), height: 16 (over x, z_hi, core).
Axes of the slice: x: 4, y: 4, z: 16 (z_hi: 2, z_lo: 8; z = z_hi * 8 + z_lo), core: 2. Of those that a mesh axis runs over, the one named last changes fastest.
Arguments:
- queries: bfloat16 [64, 48, 32, 2560], P('tm', 'height'), may hold values from -8 to 8
- keys_values: bfloat16 [2, 64, 48, 32, 2560], P(None, 'tm', 'height'), may hold values from -8 to 8
- anchor_ids: int32 [96], replicated, may hold values from 0 to 1535, as said below
Outputs:
- attended: bfloat16 [64, 48, 32, 2560], P('tm', 'height')
Inputs may be any that keep to these rules, and one draw needn't show every extreme that they name: `anchor_ids`: anchor j lies in tile j: tiles of 4 x 4 tokens of frame 0 in row-major order, 8 a tile row; the first tile's anchor is its first token and the last tile's its last token.
All inputs are finite; a program needn't handle non-finite values.
Results may differ from a plain program's by a relative error of at most 0.0033.
Values may be sent and summed in bfloat16 or wider, within the bound.
A program may use at most 128 MiB of HBM per device.

v0:
```python
import jax
import jax.numpy as jnp
from jax import lax
from jax.sharding import PartitionSpec as P

HEADS = 20


def with_halo(cells, sides, width):
    for axis, dim in sides:
        count = lax.axis_size(axis)
        ends = count - 1
        head = lax.slice_in_dim(cells, 0, width, axis=dim)
        tail = lax.slice_in_dim(cells, cells.shape[dim] - width, cells.shape[dim], axis=dim)
        cells = jnp.concatenate(
            [
                lax.ppermute(tail, axis, [(i, (i + 1) % count) for i in range(ends)]),
                cells,
                lax.ppermute(head, axis, [((i + 1) % count, i) for i in range(ends)]),
            ],
            axis=dim,
        )
    return cells


def per_device(queries, keys_values, anchor_ids):
    frames, rows, cols, feat = queries.shape
    heads = HEADS
    head_dim = feat // heads
    half = feat // 2
    half_heads = heads // 2
    scale = 1.0 / head_dim**0.5
    count = anchor_ids.shape[0]
    time_index = lax.axis_index("tm")
    row_index = lax.axis_index("height")
    all_frames = frames * lax.axis_size("tm")
    all_rows = rows * lax.axis_size("height")
    local_tokens = row_index * rows * cols + jnp.arange(rows * cols, dtype=jnp.int32)
    first_flat = keys_values[:, 0].reshape(2, rows * cols, feat)
    selector = (anchor_ids[:, None] == local_tokens[None, :]) & (time_index == 0)
    selector = selector.astype(jnp.bfloat16)
    picked = jnp.einsum("an,snf->saf", selector, first_flat, preferred_element_type=jnp.float32)
    anchors = lax.psum(picked, ("tm", "height")).astype(jnp.bfloat16)
    widened = with_halo(keys_values, (("tm", 1),), 1)
    padded = with_halo(widened, (("height", 2),), 3)
    span = rows + 6
    query_rows = jnp.arange(rows, dtype=jnp.int32)
    key_rows = jnp.arange(span, dtype=jnp.int32) - 3
    col_iota = jnp.arange(cols, dtype=jnp.int32)
    row_near = jnp.abs(key_rows[None, :] - query_rows[:, None]) <= 3
    col_near = jnp.abs(col_iota[None, :] - col_iota[:, None]) <= 3
    global_rows = row_index * rows + key_rows
    row_valid = (global_rows >= 0) & (global_rows < all_rows)
    relation = (
        row_near[:, None, None, :, None]
        & col_near[None, :, None, None, :]
        & row_valid[None, None, None, :, None]
    )

    def block(index):
        frame = index // 2
        group = index % 2
        zero = jnp.zeros((), jnp.int32)
        query_block = lax.dynamic_slice(
            queries, (frame, zero, zero, group * half), (1, rows, cols, half)
        )
        query_block = query_block.reshape(rows * cols, half_heads, head_dim)
        key_block = lax.dynamic_slice(
            padded, (zero, frame, zero, zero, group * half), (2, 3, span, cols, half)
        )
        key_block = key_block.reshape(2, 3 * span * cols, half_heads, head_dim)
        anchor_block = lax.dynamic_slice_in_dim(anchors, group * half, half, 2).reshape(
            2, count, half_heads, head_dim
        )
        key_frames = time_index * frames + frame - 1 + jnp.arange(3, dtype=jnp.int32)
        frame_valid = (key_frames >= 0) & (key_frames < all_frames)
        allowed = relation & frame_valid[None, None, :, None, None]
        allowed = allowed.reshape(rows * cols, 3 * span * cols)
        local_scores = (
            jnp.einsum(
                "qhd,khd->hqk", query_block, key_block[0], preferred_element_type=jnp.float32
            )
            * scale
        )
        local_scores = jnp.where(allowed[None], local_scores, -1e30)
        anchor_scores = (
            jnp.einsum(
                "qhd,ahd->hqa", query_block, anchor_block[0], preferred_element_type=jnp.float32
            )
            * scale
        )
        top = jnp.maximum(jnp.max(local_scores, axis=-1), jnp.max(anchor_scores, axis=-1))
        local_weights = jnp.exp(local_scores - top[..., None])
        anchor_weights = jnp.exp(anchor_scores - top[..., None])
        total = jnp.sum(local_weights, axis=-1) + jnp.sum(anchor_weights, axis=-1)
        summed = jnp.einsum(
            "hqk,khd->qhd",
            local_weights.astype(jnp.bfloat16),
            key_block[1],
            preferred_element_type=jnp.float32,
        )
        summed = summed + jnp.einsum(
            "hqa,ahd->qhd",
            anchor_weights.astype(jnp.bfloat16),
            anchor_block[1],
            preferred_element_type=jnp.float32,
        )
        result = summed / jnp.transpose(total)[:, :, None]
        return result.reshape(rows * cols, half).astype(jnp.bfloat16)

    blocks = lax.map(block, jnp.arange(2 * frames, dtype=jnp.int32))
    blocks = blocks.reshape(frames, 2, rows, cols, half)
    return jnp.transpose(blocks, (0, 2, 3, 1, 4)).reshape(frames, rows, cols, feat)


def solution(mesh):
    return jax.shard_map(
        per_device,
        mesh=mesh,
        in_specs=(P("tm", "height", None, None), P(None, "tm", "height", None, None), P()),
        out_specs=P("tm", "height", None, None),
        check_vma=False,
    )
```

profile of v0, /device:TPU:1, one launch (start us, length us, event | category | flops | bytes accessed | tf_op | source)
XLA Modules:
  0.0 647.8 jit_solution(9624231081286156777)
XLA Ops:
  0.0 1.8 fusion.32
  1.8 4.4 collective-permute-start
  6.3 1.3 collective-permute-start.1
  7.6 16.2 %collective-permute-done = bf16[2,1,3,32,2560]{4,3,2,1,0:T(8,128)(2,1)S(1)} collective-permute-done((bf16[2,1,3,32,2560]{4,3,2,1,0:T(8,128)(2,1)S(1)}, bf16[2,1,3,32,2560]{4,3,2,1,0:T(8,128)(2,1)S(1)}, u32[]{:S(2)}, u32[]{:S(2)}) %collective-permute-start) | collective-permute-done | bytes 983072 | tf_op jit(solution)/shard_map/ppermute | solution.py:17
  24.8 1.5 constant_dynamic-update-slice_fusion.2
  26.2 22.7 %collective-permute-done.1 = bf16[2,1,3,32,2560]{4,3,2,1,0:T(8,128)(2,1)S(1)} collective-permute-done((bf16[2,1,3,32,2560]{4,3,2,1,0:T(8,128)(2,1)S(1)}, bf16[2,1,3,32,2560]{4,3,2,1,0:T(8,128)(2,1)S(1)}, u32[]{:S(2)}, u32[]{:S(2)}) %collective-permute-start.1) | collective-permute-done | bytes 983072 | tf_op jit(solution)/shard_map/ppermute | solution.py:19
  50.0 18.9 %collective-permute-start.2 = (bf16[2,4,3,32,2560]{4,3,2,1,0:T(8,128)(2,1)}, bf16[2,4,3,32,2560]{4,3,2,1,0:T(8,128)(2,1)}, u32[]{:S(2)}, u32[]{:S(2)}) collective-permute-start(bf16[2,4,3,32,2560]{4,3,2,1,0:T(8,128)(2,1)} %constant_dynamic-update-slice_fusion.1), channel_id=1, source_target_pairs={{0,1},{1,2},{2,3},{3,4},{4,5},{5,6},{6,7},{7,8},{8,9},{9,10},{10,1... | collective-permute-start | bytes 11796488 | tf_op jit(solution)/shard_map/ppermute | solution.py:17
  68.9 1.9 collective-permute-start.3
  71.4 412.8 %all-reduce.1 = bf16[2,96,2560]{2,1,0:T(8,128)(2,1)} all-reduce(f32[2,96,2560]{2,1,0:T(8,128)S(1)} %convolution_bitcast_fusion), channel_id=1, replica_groups=mesh['tm'=32,'height'=16] {'tm','height'}, use_global_device_ids=true, to_apply=%region_0.0 | all-reduce | flops 491520 | bytes 2949120 | tf_op jit(solution)/shard_map/psum | solution.py:43
  484.3 10.5 %pad_maximum_fusion = bf16[2,4,9,32,2560]{4,3,2,1,0:T(8,128)(2,1)} fusion(bf16[2,4,3,32,2560]{4,3,2,1,0:T(8,128)(2,1)} %collective-permute-done.3, bf16[2,4,3,32,2560]{4,3,2,1,0:T(8,128)(2,1)} %constant_dynamic-update-slice_fusion.1, bf16[2,4,3,32,2560]{4,3,2,1,0:T(8,128)(2,1)} %collective-permute-done.2), kind=kLoop, calls=%fused_computation.37 | loop fusion | flops 11796480 | bytes 23592960 | tf_op jit(solution)/shard_map/concatenate | solution.py:15
  495.2 150.3 %while.14 = (s32[]{:T(128)}, bf16[4,96,1280]{2,1,0:T(8,128)(2,1)}, s32[4]{0:T(128)}, bf16[2,4,9,32,2560]{4,3,2,1,0:T(8,128)(2,1)}, s32[]{:T(128)}, /*index=5*/bf...) while((s32[]{:T(128)}, bf16[4,96,1280]{2,1,0:T(8,128)(2,1)}, ...), condition=%wide.region_6.7_spmd.clone, body=%wide.region_1.6_spmd.clone.sunk | while | flops 482041024 | bytes 46167800 | solution.py:111
  495.2 1.3 dynamic_slice.37
  499.1 3.9 constant_dynamic-slice_fusion.8
  503.0 2.9 squeeze.44
  509.6 4.1 fusion.52
  514.5 1.8 copy.77
  516.3 1.4 fusion.53
  518.8 5.5 squeeze.43
  524.3 4.7 fusion.54
  530.1 1.6 fusion.57
  532.8 1.3 dynamic_slice.37
  536.7 3.9 constant_dynamic-slice_fusion.8
  540.6 2.9 squeeze.44
  547.1 4.1 fusion.52
  552.1 1.8 copy.77
  553.9 1.4 fusion.53
  556.4 5.5 squeeze.43
  561.9 4.7 fusion.54
  567.7 1.6 fusion.57
  570.4 1.3 dynamic_slice.37
  574.3 3.9 constant_dynamic-slice_fusion.8
  578.2 2.9 squeeze.44
  584.7 4.1 fusion.52
  589.7 1.8 copy.77
  591.5 1.4 fusion.53
  594.0 5.5 squeeze.43
  599.5 4.7 fusion.54
  605.3 1.6 fusion.57
  608.0 1.3 dynamic_slice.37
  611.9 3.9 constant_dynamic-slice_fusion.8
  615.8 2.9 squeeze.44
  622.3 4.1 fusion.52
  627.2 1.8 copy.77
  629.1 1.4 fusion.53
  631.6 5.5 squeeze.43
  637.0 4.7 fusion.54
  642.9 1.6 fusion.57
  645.6 2.2 copy.48
  (108 shorter events, 34.2 us)
Async XLA Ops:
  0.0 24.8 %copy-start.2 = (bf16[2,2,3,32,2560]{4,3,2,1,0:T(8,128)(2,1)S(1)}, bf16[2,2,3,32,2560]{4,3,2,1,0:T(8,128)(2,1)}, u32[]{:S(2)}) copy-start(bf16[2,2,3,32,2560]{4,3,2,1,0:T(8,128)(2,1)} %param.6) | copy-start | bytes 5898244
  1.8 21.9 %collective-permute-start = (bf16[2,1,3,32,2560]{4,3,2,1,0:T(8,128)(2,1)S(1)}, bf16[2,1,3,32,2560]{4,3,2,1,0:T(8,128)(2,1)S(1)}, u32[]{:S(2)}, u32[]{:S(2)}) collective-permute-start(bf16[2,1,3,32,2560]{4,3,2,1,0:T(8,128)(2,1)S(1)} %get-tuple-element.226), channel_id=1, source_target_pairs={{0,16},{16,32},{32,48},{48,64},{64,80},{80,96},{96,112},{112,128},... | collective-permute-start | bytes 2949128 | tf_op jit(solution)/shard_map/ppermute | solution.py:17
  6.3 42.7 %collective-permute-start.1 = (bf16[2,1,3,32,2560]{4,3,2,1,0:T(8,128)(2,1)S(1)}, bf16[2,1,3,32,2560]{4,3,2,1,0:T(8,128)(2,1)S(1)}, u32[]{:S(2)}, u32[]{:S(2)}) collective-permute-start(bf16[2,1,3,32,2560]{4,3,2,1,0:T(8,128)(2,1)S(1)} %get-tuple-element.225), channel_id=1, source_target_pairs={{16,0},{32,16},{48,32},{64,48},{80,64},{96,80},{112,96},{128,112},... | collective-permute-start | bytes 2949128 | tf_op jit(solution)/shard_map/ppermute | solution.py:19
  24.8 46.1 %copy-start.3 = (s32[96]{0:T(128)S(1)}, s32[96]{0:T(128)}, u32[]{:S(2)}) copy-start(s32[96]{0:T(128)} %param.7) | copy-start | bytes 1156
  50.0 434.3 %collective-permute-start.2 = (bf16[2,4,3,32,2560]{4,3,2,1,0:T(8,128)(2,1)}, bf16[2,4,3,32,2560]{4,3,2,1,0:T(8,128)(2,1)}, u32[]{:S(2)}, u32[]{:S(2)}) collective-permute-start(bf16[2,4,3,32,2560]{4,3,2,1,0:T(8,128)(2,1)} %constant_dynamic-update-slice_fusion.1), channel_id=1, source_target_pairs={{0,1},{1,2},{2,3},{3,4},{4,5},{5,6},{6,7},{7,8},{8,9},{9,10},{10,1... | collective-permute-start | bytes 11796488 | tf_op jit(solution)/shard_map/ppermute | solution.py:17
  68.9 415.4 %collective-permute-start.3 = (bf16[2,4,3,32,2560]{4,3,2,1,0:T(8,128)(2,1)}, bf16[2,4,3,32,2560]{4,3,2,1,0:T(8,128)(2,1)}, u32[]{:S(2)}, u32[]{:S(2)}) collective-permute-start(bf16[2,4,3,32,2560]{4,3,2,1,0:T(8,128)(2,1)} %constant_dynamic-update-slice_fusion.1), channel_id=1, source_target_pairs={{1,0},{2,1},{3,2},{4,3},{5,4},{6,5},{7,6},{8,7},{9,8},{10,9},{11,1... | collective-permute-start | bytes 11796488 | tf_op jit(solution)/shard_map/ppermute | solution.py:19
  509.6 4.1 copy-start.1
  517.7 0.9 copy-start
  547.1 4.1 copy-start.1
  555.3 0.9 copy-start
  584.7 4.1 copy-start.1
  592.9 0.9 copy-start
  622.3 4.1 copy-start.1
  630.5 0.9 copy-start
where the time goes:
time: 649 us; the launch traced here: 648 us
  blocking collectives  413 us (64%)
  local copies, waits for them, and re-layouts  94.9 us (15%)
  matrix products  47.4 us (7%)
  waiting for transfers between devices  38.8 us (6%)
  starting transfers between devices  26.5 us (4%)
  other arithmetic  16.4 us (3%)
  loops' own time  10.8 us (2%)
    psum x1, blocking collectives, per_device(): anchors = lax.psum(picked, ('tm', 'height')).astype(jnp.bfloat16)  413 us
    ppermute x2, starting transfers between devices, with_halo(): lax.ppermute(tail, axis, [(i, (i + 1) % count) for i in range(ends)])  23.3 us
    ppermute x2, waiting for transfers between devices, with_halo(): lax.ppermute(head, axis, [((i + 1) % count, i) for i in range(ends)])  22.7 us
    squeeze x4, local copies, waits for them, and re-layouts, block(): key_block[1]  21.9 us
    dot_general x4, matrix products, block(): jnp.einsum('hqk,khd->qhd', local_weights.astype(jnp.bfloat16), key_block[...  18.7 us
    dot_general x4, matrix products, block(): jnp.einsum('qhd,khd->hqk', query_block, key_block[0], preferred_element_t...  16.3 us
    ppermute x2, waiting for transfers between devices, with_halo(): lax.ppermute(tail, axis, [(i, (i + 1) % count) for i in range(ends)])  16.2 us
    slice x4, local copies, waits for them, and re-layouts, block(): key_block[0]  15.7 us
  transfers between devices with their start and end apart: 4, of which 2 were waited for; matrix products, arithmetic and copies ran while one was open for 0% of the time, Pallas kernels for 0%

commit v1 on v0

v1 whole, which is shorter than its diff:
```python
import functools

import jax
import jax.numpy as jnp
from jax import lax
from jax.experimental import pallas as pl
from jax.experimental.pallas import tpu as pltpu
from jax.sharding import PartitionSpec as P

HEADS = 20
GROUPS = 5
REACH = 3
LOG2E = 1.4426950408889634
MASKED = -1e30
MESH = pl.DeviceIdType.MESH

CORE, UP, DOWN, PASS_UP, PASS_DOWN, QUERY = 0, 2, 4, 6, 8, 10
PART = QUERY + GROUPS
STAT = PART + GROUPS
TRANSFERS = STAT + GROUPS


def attention_kernel(
    frames, rows, cols, tm_count, height_count,
    queries, keys_values, anchors, out,
    own, mate, own_queries, far_queries, sent_part, far_part, sent_stat, far_stat,
    result, own_level, near_bias, cross_bias, stat_block, send_sem, recv_sem, local_sem,
):
    band = rows * cols
    tokens = frames * band
    feat = queries.shape[1]
    size = feat // HEADS
    per_group = HEADS // GROUPS
    width = per_group * size
    scale = LOG2E / size**0.5

    time_index = lax.axis_index("tm")
    height_index = lax.axis_index("height")
    core = lax.rem(height_index, 2)
    has_down = time_index > 0
    has_up = time_index < tm_count - 1
    has_far = ((core == 0) & (height_index > 0)) | ((core == 1) & (height_index < height_count - 1))
    core_mate = (time_index, height_index + 1 - 2 * core)
    far_mate = (time_index, jnp.clip(height_index - 1 + 2 * core, 0, height_count - 1))
    below = (jnp.maximum(time_index - 1, 0), height_index)
    above = (jnp.minimum(time_index + 1, tm_count - 1), height_index)

    barrier = pltpu.get_barrier_semaphore()
    pl.semaphore_signal(barrier, inc=1, device_id=core_mate, device_id_type=MESH)
    for exists, mate_id in ((has_down, below), (has_up, above), (has_far, far_mate)):

        @pl.when(exists)
        def _():
            pl.semaphore_signal(barrier, inc=1, device_id=mate_id, device_id_type=MESH)

    peers = 1 + sum(exists.astype(jnp.int32) for exists in (has_down, has_up, has_far))
    pl.semaphore_wait(barrier, peers)

    def remote(index, src, dst, device):
        return pltpu.make_async_remote_copy(
            src_ref=src, dst_ref=dst, send_sem=send_sem.at[index], recv_sem=recv_sem.at[index],
            device_id=device, device_id_type=MESH,
        )

    first, last = pl.ds(0, band), pl.ds(tokens + band, band)
    middle = pl.ds(band, tokens)

    def share(kv):
        return remote(CORE + kv, keys_values.at[kv], mate.at[kv, middle], core_mate)

    def send_up(kv):
        src = keys_values.at[kv, pl.ds(tokens - band, band)]
        return remote(UP + kv, src, own.at[kv, first], above)

    def send_down(kv):
        return remote(DOWN + kv, keys_values.at[kv, pl.ds(0, band)], own.at[kv, last], below)

    def pass_first(kv):
        return remote(PASS_UP + kv, own.at[kv, first], mate.at[kv, first], core_mate)

    def pass_last(kv):
        return remote(PASS_DOWN + kv, own.at[kv, last], mate.at[kv, last], core_mate)

    def columns(group):
        return pl.ds(group * width, width)

    def send_query(group):
        cut = columns(group)
        return remote(QUERY + group, queries.at[:, cut], far_queries.at[:, cut], far_mate)

    def send_part(group):
        cut = columns(group)
        return remote(PART + group, sent_part.at[:, cut], far_part.at[:, cut], far_mate)

    def send_stat(group):
        return remote(STAT + group, sent_stat.at[group], far_stat.at[group], far_mate)

    copies = [pltpu.make_async_copy(queries, own_queries, local_sem.at[2])]
    for kv in range(2):
        copies.append(
            pltpu.make_async_copy(keys_values.at[kv], own.at[kv, middle], local_sem.at[kv])
        )
    for copy in copies:
        copy.start()
    for kv in range(2):
        share(kv).start()

    @pl.when(has_up)
    def _():
        for kv in range(2):
            send_up(kv).start()

    @pl.when(has_down)
    def _():
        for kv in range(2):
            send_down(kv).start()

    @pl.when(has_far)
    def _():
        for group in range(GROUPS):
            send_query(group).start()

    @pl.when(jnp.logical_not(has_down))
    def _():
        for ref in (own, mate):
            ref[:, 0:band, :] = jnp.zeros((2, band, feat), ref.dtype)

    @pl.when(jnp.logical_not(has_up))
    def _():
        for ref in (own, mate):
            ref[:, tokens + band : tokens + 2 * band, :] = jnp.zeros((2, band, feat), ref.dtype)

    @pl.when(jnp.logical_not(has_far))
    def _():
        far_part[...] = jnp.zeros(far_part.shape, far_part.dtype)
        far_stat[...] = jnp.full(far_stat.shape, MASKED, far_stat.dtype)

    span = 3 * band
    query_token = lax.broadcasted_iota(jnp.int32, (band, span), 0)
    key_token = lax.broadcasted_iota(jnp.int32, (band, span), 1)
    query_row, query_col = query_token // cols, lax.rem(query_token, cols)
    key_frame = key_token // band
    key_row = lax.rem(key_token, band) // cols
    key_col = lax.rem(key_token, cols)
    near = jnp.abs(query_col - key_col) <= REACH
    behind = jnp.where(core == 0, query_row - key_row, key_row - query_row)
    for frame in range(frames):
        moment = time_index * frames + frame - 1 + key_frame
        valid = near & (moment >= 0) & (moment < tm_count * frames)
        near_bias[frame] = jnp.where(valid, 0.0, MASKED)
        cross_bias[frame] = jnp.where(valid & (behind >= 0), 0.0, MASKED)

    @pl.when(has_down)
    def _():
        for kv in range(2):
            send_up(kv).wait_recv()
            pass_first(kv).start()

    @pl.when(has_up)
    def _():
        for kv in range(2):
            send_down(kv).wait_recv()
            pass_last(kv).start()

    for copy in copies:
        copy.wait()

    def scores(query, keys):
        return scale * lax.dot_general(
            query, keys, (((1,), (1,)), ((), ())), preferred_element_type=jnp.float32
        )

    def weighted(weights, values):
        return jnp.dot(weights.astype(values.dtype), values, preferred_element_type=jnp.float32)

    lane = lax.broadcasted_iota(jnp.int32, (band, size), 1)

    def far_block(group, step):
        head, frame = step // frames, lax.rem(step, frames)
        cut = pl.ds(pl.multiple_of((group * per_group + head) * size, size), size)
        here = pl.ds(pl.multiple_of(frame * band, band), band)
        around = pl.ds(pl.multiple_of(frame * band, band), span)
        score = scores(far_queries[here, cut], own[0, around, cut]) + cross_bias[frame]
        top = jnp.max(score, axis=1, keepdims=True)
        weights = jnp.exp2(score - top)
        total = jnp.sum(weights, axis=1, keepdims=True)
        part = weighted(weights, own[1, around, cut]) / total
        sent_part[here, cut] = part.astype(sent_part.dtype)
        level = top + jnp.log(total) * LOG2E
        stat_block[here, :] = jnp.where(lane == head, level, stat_block[here, :])

    @pl.when(has_far)
    def _():
        stat_block[...] = jnp.zeros(stat_block.shape, stat_block.dtype)
        for group in range(GROUPS):
            send_query(group).wait_recv()

            @pl.loop(0, frames * per_group)
            def _(step):
                far_block(group, step)

            sent_stat[group] = jnp.transpose(stat_block[...])[0:8]
            send_part(group).start()
            send_stat(group).start()

    for kv in range(2):
        share(kv).wait_recv()

    @pl.when(has_down)
    def _():
        for kv in range(2):
            pass_first(kv).wait_recv()

    @pl.when(has_up)
    def _():
        for kv in range(2):
            pass_last(kv).wait_recv()

    @pl.loop(0, frames * HEADS)
    def _(step):
        head, frame = step // frames, lax.rem(step, frames)
        cut = pl.ds(pl.multiple_of(head * size, size), size)
        here = pl.ds(pl.multiple_of(frame * band, band), band)
        around = pl.ds(pl.multiple_of(frame * band, band), span)
        query = own_queries[here, cut]
        near_score = scores(query, own[0, around, cut]) + near_bias[frame]
        cross_score = scores(query, mate[0, around, cut]) + cross_bias[frame]
        anchor_score = scores(query, anchors[0, :, cut])
        top = jnp.maximum(
            jnp.maximum(
                jnp.max(near_score, axis=1, keepdims=True),
                jnp.max(cross_score, axis=1, keepdims=True),
            ),
            jnp.max(anchor_score, axis=1, keepdims=True),
        )
        near_weights = jnp.exp2(near_score - top)
        cross_weights = jnp.exp2(cross_score - top)
        anchor_weights = jnp.exp2(anchor_score - top)
        total = (
            jnp.sum(near_weights, axis=1, keepdims=True)
            + jnp.sum(cross_weights, axis=1, keepdims=True)
            + jnp.sum(anchor_weights, axis=1, keepdims=True)
        )
        summed = (
            weighted(near_weights, own[1, around, cut])
            + weighted(cross_weights, mate[1, around, cut])
            + weighted(anchor_weights, anchors[1, :, cut])
        )
        result[here, cut] = summed / total
        own_level[here, cut] = jnp.broadcast_to(top + jnp.log(total) * LOG2E, (band, size))

    for group in range(GROUPS):

        @pl.when(has_far)
        def _():
            send_part(group).wait_recv()
            send_stat(group).wait_recv()

        stats = jnp.transpose(far_stat[group])
        for head in range(per_group):
            cut = pl.ds((group * per_group + head) * size, size)
            far_level = stats[0:tokens, head : head + 1]
            mine = own_level[:, cut]
            top = jnp.maximum(mine, far_level)
            mine = jnp.exp2(mine - top)
            other = jnp.exp2(far_level - top)
            mixed = mine * result[:, cut] + other * far_part[:, cut].astype(jnp.float32)
            out[:, cut] = (mixed / (mine + other)).astype(out.dtype)

    for kv in range(2):
        share(kv).wait_send()

    @pl.when(has_up)
    def _():
        for kv in range(2):
            send_up(kv).wait_send()
            pass_last(kv).wait_send()

    @pl.when(has_down)
    def _():
        for kv in range(2):
            send_down(kv).wait_send()
            pass_first(kv).wait_send()

    @pl.when(has_far)
    def _():
        for group in range(GROUPS):
            send_query(group).wait_send()
            send_part(group).wait_send()
            send_stat(group).wait_send()


def per_device(tm_count, height_count, queries, keys_values, anchor_ids):
    frames, rows, cols, feat = queries.shape
    band = rows * cols
    tokens = frames * band
    size = feat // HEADS
    padded = -(-tokens // 128) * 128
    time_index = lax.axis_index("tm")
    row_index = lax.axis_index("height")
    local_tokens = row_index * band + jnp.arange(band, dtype=jnp.int32)
    first_flat = keys_values[:, 0].reshape(2, band, feat)
    selector = (anchor_ids[:, None] == local_tokens[None, :]) & (time_index == 0)
    selector = selector.astype(jnp.bfloat16)
    picked = jnp.einsum("an,snf->saf", selector, first_flat, preferred_element_type=jnp.float32)
    anchors = lax.psum(picked, ("tm", "height")).astype(jnp.bfloat16)

    kernel = functools.partial(attention_kernel, frames, rows, cols, tm_count, height_count)
    bf16, f32 = jnp.bfloat16, jnp.float32
    out = pl.pallas_call(
        kernel,
        out_shape=jax.ShapeDtypeStruct((tokens, feat), bf16),
        in_specs=[
            pl.BlockSpec(memory_space=pl.ANY),
            pl.BlockSpec(memory_space=pl.ANY),
            pl.BlockSpec(memory_space=pltpu.VMEM),
        ],
        out_specs=pl.BlockSpec(memory_space=pltpu.VMEM),
        scratch_shapes=[
            pltpu.VMEM((2, tokens + 2 * band, feat), bf16),
            pltpu.VMEM((2, tokens + 2 * band, feat), bf16),
            pltpu.VMEM((tokens, feat), bf16),
            pltpu.VMEM((tokens, feat), bf16),
            pltpu.VMEM((tokens, feat), bf16),
            pltpu.VMEM((tokens, feat), bf16),
            pltpu.VMEM((GROUPS, 8, padded), f32),
            pltpu.VMEM((GROUPS, 8, padded), f32),
            pltpu.VMEM((tokens, feat), f32),
            pltpu.VMEM((tokens, feat), f32),
            pltpu.VMEM((frames, band, 3 * band), f32),
            pltpu.VMEM((frames, band, 3 * band), f32),
            pltpu.VMEM((padded, size), f32),
            pltpu.SemaphoreType.DMA((TRANSFERS,)),
            pltpu.SemaphoreType.DMA((TRANSFERS,)),
            pltpu.SemaphoreType.DMA((3,)),
        ],
        compiler_params=pltpu.CompilerParams(
            collective_id=0, has_side_effects=True, vmem_limit_bytes=48 * 1024 * 1024
        ),
        name="attention",
    )(queries.reshape(tokens, feat), keys_values.reshape(2, tokens, feat), anchors)
    return out.reshape(frames, rows, cols, feat)


def solution(mesh):
    body = functools.partial(per_device, mesh.shape["tm"], mesh.shape["height"])
    return jax.shard_map(
        body,
        mesh=mesh,
        in_specs=(P("tm", "height", None, None), P(None, "tm", "height", None, None), P()),
        out_specs=P("tm", "height", None, None),
        check_vma=False,
    )
```

time: 649 us -> 377 us (0.58)
  the two profiles are of different devices: /device:TPU:1 before, /device:TPU:90 now
where the time goes in v1:
time: 377 us
  Pallas kernels  260 us (69%)
  blocking collectives  112 us (30%)
    pallas_call x1, Pallas kernels, per_device(): pl.pallas_call(kernel, out_shape=jax.ShapeDtypeStruct((tokens, feat), bf1...  260 us
    psum x1, blocking collectives, per_device(): anchors = lax.psum(picked, ('tm', 'height')).astype(jnp.bfloat16)  112 us

profile of v1, /device:TPU:90, one launch (start us, length us, event | category | flops | bytes accessed | tf_op | source)
XLA Modules:
  0.0 376.9 jit_solution(4585184226957674730)
XLA Ops:
  0.0 0.0 copy-start.2
  0.0 1.3 slice.3
  1.3 0.0 copy-done.2
  1.3 1.8 convolution_bitcast_fusion
  3.1 0.0 copy-start
  3.1 111.6 %all-reduce.1.anchors = bf16[2,96,2560]{2,1,0:T(8,128)(2,1)S(1)} all-reduce(f32[2,96,2560]{2,1,0:T(8,128)} %convolution_bitcast_fusion), channel_id=1, replica_groups=mesh['tm'=32,'height'=16] {'tm','height'}, use_global_device_ids=true, to_apply=%region_0.0 | all-reduce | flops 491520 | bytes 2949120 | tf_op jit(solution)/shard_map/psum | solution.py:306
  114.7 0.0 copy-done
  114.7 0.0 copy-start.1
  114.7 1.2 copy-done.1
  115.9 260.0 %attention.1 = bf16[192,2560]{1,0:T(8,128)(2,1)S(1)} custom-call(bf16[192,2560]{1,0:T(8,128)(2,1)S(1)} %bitcast.12, bf16[2,192,2560]{2,1,0:T(8,128)(2,1)S(1)} %bitcast.10, bf16[2,96,2560]{2,1,0:T(8,128)(2,1)S(1)} %all-reduce.1.anchors), custom_call_target="tpu_custom_call" | custom-call | tf_op jit(solution)/shard_map/attention/pallas_call | solution.py:310
  375.9 0.9 copy.7
  (1 shorter events, 0.0 us)
Async XLA Ops:
  0.0 1.3 copy-start.2
  3.1 111.6 %copy-start = (bf16[2,2,3,32,2560]{4,3,2,1,0:T(8,128)(2,1)S(1)}, bf16[2,2,3,32,2560]{4,3,2,1,0:T(8,128)(2,1)}, u32[]{:S(2)}) copy-start(bf16[2,2,3,32,2560]{4,3,2,1,0:T(8,128)(2,1)} %param.4) | copy-start | bytes 5898244
  114.7 1.2 copy-start.1

commit v2 on v1

--- a/solution.py
+++ b/solution.py
@@ -17,14 +17,24 @@
 CORE, UP, DOWN, PASS_UP, PASS_DOWN, QUERY = 0, 2, 4, 6, 8, 10
 PART = QUERY + GROUPS
 STAT = PART + GROUPS
-TRANSFERS = STAT + GROUPS
+JOIN = STAT + GROUPS
+SCATTER = JOIN + 2
+SPREAD = SCATTER + 4
+ALONG_Y = SPREAD + 8
+ALONG_X = ALONG_Y + 4
+TO_MATE = ALONG_X + 4
+TRANSFERS = TO_MATE + 4
+
+XS, YS, Z_LO = 4, 4, 8
+SLOT = 32
 
 
 def attention_kernel(
     frames, rows, cols, tm_count, height_count,
-    queries, keys_values, anchors, out,
+    queries, keys_values, anchor_ids, out,
     own, mate, own_queries, far_queries, sent_part, far_part, sent_stat, far_stat,
-    result, own_level, near_bias, cross_bias, stat_block, send_sem, recv_sem, local_sem,
+    result, own_level, near_bias, cross_bias, stat_block,
+    partial, mate_partial, far_partial, picked, anchors, send_sem, recv_sem, local_sem,
 ):
     band = rows * cols
     tokens = frames * band
@@ -45,6 +55,28 @@
     below = (jnp.maximum(time_index - 1, 0), height_index)
     above = (jnp.minimum(time_index + 1, tm_count - 1), height_index)
 
+    x, z_hi = height_index // 4, lax.rem(height_index // 2, 2)
+    y, z_lo = time_index // Z_LO, lax.rem(time_index, Z_LO)
+    source_hi = jnp.where(z_lo < Z_LO // 2, z_hi, 1 - z_hi)
+    active = core == 1 - source_hi
+    hub = active & (z_lo == 0)
+    root = time_index == 0
+    face = hub & root
+    leaf = active & (z_lo != 0)
+    y_peers = [(lax.rem(y + d, YS) * Z_LO + z_lo, height_index) for d in range(1, YS)]
+    x_peers = [
+        (time_index, (lax.rem(x + d, XS) * 2 + z_hi) * 2 + core) for d in range(1, XS)
+    ]
+
+    def at_z(z):
+        return (y * Z_LO + lax.rem(z, Z_LO), (x * 2 + z // Z_LO) * 2 + core)
+
+    leaves = [
+        at_z(lax.rem(z_hi * Z_LO + d + 2 * Z_LO, 2 * Z_LO))
+        for d in (-4, 3, -3, 2, -2, 1, -1)
+    ]
+    my_hub = at_z(source_hi * Z_LO)
+
     barrier = pltpu.get_barrier_semaphore()
     pl.semaphore_signal(barrier, inc=1, device_id=core_mate, device_id_type=MESH)
     for exists, mate_id in ((has_down, below), (has_up, above), (has_far, far_mate)):
@@ -53,12 +85,21 @@
         def _():
             pl.semaphore_signal(barrier, inc=1, device_id=mate_id, device_id_type=MESH)
 
-    peers = 1 + sum(exists.astype(jnp.int32) for exists in (has_down, has_up, has_far))
+    for exists, group in ((active, y_peers + x_peers), (hub, leaves), (leaf, [my_hub])):
+
+        @pl.when(exists)
+        def _():
+            for mate_id in group:
+                pl.semaphore_signal(barrier, inc=1, device_id=mate_id, device_id_type=MESH)
+
+    peers = 1 + sum(exists.astype(jnp.int32) for exists in (has_down, has_up, has_far, leaf))
+    peers = peers + 6 * active.astype(jnp.int32) + 7 * hub.astype(jnp.int32)
     pl.semaphore_wait(barrier, peers)
 
-    def remote(index, src, dst, device):
+    def remote(index, src, dst, device, arrival=None):
+        arrival = index if arrival is None else arrival
         return pltpu.make_async_remote_copy(
-            src_ref=src, dst_ref=dst, send_sem=send_sem.at[index], recv_sem=recv_sem.at[index],
+            src_ref=src, dst_ref=dst, send_sem=send_sem.at[index], recv_sem=recv_sem.at[arrival],
             device_id=device, device_id_type=MESH,
         )
 
@@ -94,6 +135,41 @@
 
     def send_stat(group):
         return remote(STAT + group, sent_stat.at[group], far_stat.at[group], far_mate)
+
+    def slot(index):
+        return pl.ds(pl.multiple_of(index * SLOT, SLOT), SLOT)
+
+    piece = feat // YS
+
+    def quarter(index):
+        return pl.ds(pl.multiple_of(index * piece, piece), piece)
+
+    def join_core():
+        return remote(JOIN, partial, mate_partial, core_mate)
+
+    def join_far():
+        return remote(JOIN + 1, partial, far_partial, far_mate)
+
+    def scatter(d):
+        cut = quarter(lax.rem(y + d, YS))
+        src, dst = picked.at[:, :, cut], anchors.at[:, slot(x), cut]
+        return remote(SCATTER + d, src, dst, y_peers[d - 1], SCATTER)
+
+    def spread(index):
+        here = anchors.at[:, slot(x), quarter(y)]
+        return remote(SPREAD + index, here, here, leaves[index], SPREAD)
+
+    def along_y(d, arriving=False):
+        here = anchors.at[:, slot(x), quarter(lax.rem(y + YS - d, YS) if arriving else y)]
+        return remote(ALONG_Y + d, here, here, y_peers[d - 1])
+
+    def along_x(d, arriving=False):
+        here = anchors.at[:, slot(lax.rem(x + XS - d, XS) if arriving else x)]
+        return remote(ALONG_X + d, here, here, x_peers[d - 1])
+
+    def to_mate(d):
+        here = anchors.at[:, slot(lax.rem(x + XS - d, XS))]
+        return remote(TO_MATE + d, here, here, core_mate)
 
     copies = [pltpu.make_async_copy(queries, own_queries, local_sem.at[2])]
     for kv in range(2):
@@ -119,6 +195,63 @@
     def _():
         for group in range(GROUPS):
             send_query(group).start()
+
+    @pl.when(root)
+    def _():
+        for kv in range(2):
+            copies[1 + kv].wait()
+        ids = anchor_ids[slot(x), :]
+        token = lax.broadcasted_iota(jnp.int32, (SLOT, band), 1) + height_index * band
+        selector = (ids[:, 0:band] == token).astype(partial.dtype)
+        for kv in range(2):
+            for part in range(YS):
+                cut = slice(part * piece, (part + 1) * piece)
+                partial[kv, :, cut] = jnp.dot(
+                    selector, own[kv, band : 2 * band, cut], preferred_element_type=jnp.float32
+                ).astype(partial.dtype)
+        join_core().start()
+        join_core().wait()
+        for kv in range(2):
+            picked[kv] = partial[kv] + mate_partial[kv]
+
+    @pl.when(face)
+    def _():
+        for kv in range(2):
+            partial[kv] = picked[kv]
+        join_far().start()
+        join_far().wait()
+        for kv in range(2):
+            picked[kv] = picked[kv] + far_partial[kv]
+        for d in range(1, YS):
+            scatter(d).start()
+        anchors[:, slot(x), 0:piece] = picked[:, :, 0:piece]
+
+    @pl.when(hub & jnp.logical_not(root))
+    def _():
+        scatter_arrived = anchors.at[:, slot(x), quarter(y)]
+        remote(SCATTER, scatter_arrived, scatter_arrived, y_peers[0]).wait_recv()
+
+    @pl.when(hub)
+    def _():
+        for index in range(7):
+            spread(index).start()
+
+    @pl.when(leaf)
+    def _():
+        spread(0).wait_recv()
+
+    @pl.when(active)
+    def _():
+        for d in range(1, YS):
+            along_y(d).start()
+        for d in range(1, YS):
+            along_y(d, True).wait_recv()
+        for d in range(1, XS):
+            along_x(d).start()
+        to_mate(0).start()
+        for d in range(1, XS):
+            along_x(d, True).wait_recv()
+            to_mate(d).start()
 
     @pl.when(jnp.logical_not(has_down))
     def _():
@@ -162,8 +295,12 @@
             send_down(kv).wait_recv()
             pass_last(kv).start()
 
-    for copy in copies:
-        copy.wait()
+    copies[0].wait()
+
+    @pl.when(jnp.logical_not(root))
+    def _():
+        for kv in range(2):
+            copies[1 + kv].wait()
 
     def scores(query, keys):
         return scale * lax.dot_general(
@@ -216,6 +353,14 @@
         for kv in range(2):
             pass_last(kv).wait_recv()
 
+    @pl.when(jnp.logical_not(active))
+    def _():
+        for d in range(XS):
+            to_mate(d).wait_recv()
+
+    held = lax.rem(lax.broadcasted_iota(jnp.int32, (1, XS * SLOT), 1), SLOT)
+    anchor_bias = jnp.where(held < 24, 0.0, MASKED)
+
     @pl.loop(0, frames * HEADS)
     def _(step):
         head, frame = step // frames, lax.rem(step, frames)
@@ -225,7 +370,7 @@
         query = own_queries[here, cut]
         near_score = scores(query, own[0, around, cut]) + near_bias[frame]
         cross_score = scores(query, mate[0, around, cut]) + cross_bias[frame]
-        anchor_score = scores(query, anchors[0, :, cut])
+        anchor_score = scores(query, anchors[0, :, cut]) + anchor_bias
         top = jnp.maximum(
             jnp.maximum(
                 jnp.max(near_score, axis=1, keepdims=True),
@@ -282,6 +427,25 @@
             send_down(kv).wait_send()
             pass_first(kv).wait_send()
 
+    @pl.when(face)
+    def _():
+        for d in range(1, YS):
+            scatter(d).wait_send()
+
+    @pl.when(hub)
+    def _():
+        for index in range(7):
+            spread(index).wait_send()
+
+    @pl.when(active)
+    def _():
+        for d in range(1, YS):
+            along_y(d).wait_send()
+        for d in range(1, XS):
+            along_x(d).wait_send()
+        for d in range(XS):
+            to_mate(d).wait_send()
+
     @pl.when(has_far)
     def _():
         for group in range(GROUPS):
@@ -296,14 +460,8 @@
     tokens = frames * band
     size = feat // HEADS
     padded = -(-tokens // 128) * 128
-    time_index = lax.axis_index("tm")
-    row_index = lax.axis_index("height")
-    local_tokens = row_index * band + jnp.arange(band, dtype=jnp.int32)
-    first_flat = keys_values[:, 0].reshape(2, band, feat)
-    selector = (anchor_ids[:, None] == local_tokens[None, :]) & (time_index == 0)
-    selector = selector.astype(jnp.bfloat16)
-    picked = jnp.einsum("an,snf->saf", selector, first_flat, preferred_element_type=jnp.float32)
-    anchors = lax.psum(picked, ("tm", "height")).astype(jnp.bfloat16)
+    ids = jnp.pad(anchor_ids.reshape(XS, -1), ((0, 0), (0, SLOT - 24)), constant_values=-1)
+    ids = jnp.broadcast_to(ids.reshape(XS * SLOT, 1), (XS * SLOT, 128))
 
     kernel = functools.partial(attention_kernel, frames, rows, cols, tm_count, height_count)
     bf16, f32 = jnp.bfloat16, jnp.float32
@@ -330,6 +488,11 @@
             pltpu.VMEM((frames, band, 3 * band), f32),
             pltpu.VMEM((frames, band, 3 * band), f32),
             pltpu.VMEM((padded, size), f32),
+            pltpu.VMEM((2, SLOT, feat), bf16),
+            pltpu.VMEM((2, SLOT, feat), bf16),
+            pltpu.VMEM((2, SLOT, feat), bf16),
+            pltpu.VMEM((2, SLOT, feat), bf16),
+            pltpu.VMEM((2, XS * SLOT, feat), bf16),
             pltpu.SemaphoreType.DMA((TRANSFERS,)),
             pltpu.SemaphoreType.DMA((TRANSFERS,)),
             pltpu.SemaphoreType.DMA((3,)),
@@ -338,7 +501,7 @@
             collective_id=0, has_side_effects=True, vmem_limit_bytes=48 * 1024 * 1024
         ),
         name="attention",
-    )(queries.reshape(tokens, feat), keys_values.reshape(2, tokens, feat), anchors)
+    )(queries.reshape(tokens, feat), keys_values.reshape(2, tokens, feat), ids)
     return out.reshape(frames, rows, cols, feat)
 
 

time: 377 us -> 251 us (0.67)
  the two profiles are of different devices: /device:TPU:90 before, /device:TPU:162 now
where the time goes in v2:
time: 251 us
  Pallas kernels  246 us (98%)
  local copies, waits for them, and re-layouts  4.6 us (2%)
    pallas_call x1, Pallas kernels, per_device(): pl.pallas_call(kernel, out_shape=jax.ShapeDtypeStruct((tokens, feat), bf1...  246 us

profile of v2, /device:TPU:162, one launch (start us, length us, event | category | flops | bytes accessed | tf_op | source)
XLA Modules:
  0.0 251.1 jit_solution(6024779882116030133)
XLA Ops:
  0.0 0.7 reshape.16
  0.7 0.1 broadcast_in_dim.7
  0.8 0.1 broadcast_in_dim.8.anchor_ids
  0.9 0.0 copy-start
  0.9 1.5 copy-done
  2.5 0.0 copy-start.1
  2.5 1.2 copy-done.1
  3.7 246.5 %attention.1 = bf16[192,2560]{1,0:T(8,128)(2,1)S(1)} custom-call(bf16[192,2560]{1,0:T(8,128)(2,1)S(1)} %bitcast.5, bf16[2,192,2560]{2,1,0:T(8,128)(2,1)S(1)} %bitcast.4, s32[128,128]{1,0:T(8,128)S(1)} %broadcast_in_dim.8.anchor_ids), custom_call_target="tpu_custom_call" | custom-call | tf_op jit(solution)/shard_map/attention/pallas_call | solution.py:468
  250.2 0.9 copy.5
  (1 shorter events, 0.0 us)
Async XLA Ops:
  0.9 1.6 copy-start
  2.5 1.2 copy-start.1

commit v3 on v2

--- a/solution.py
+++ b/solution.py
@@ -55,10 +55,18 @@
     below = (jnp.maximum(time_index - 1, 0), height_index)
     above = (jnp.minimum(time_index + 1, tm_count - 1), height_index)
 
+    bent = ((height_index == 4) | (height_index == height_count - 5))
+    turn = jnp.logical_not(has_far)
+    bend_end = (height_index == 3) | (height_index == height_count - 4)
+    low = height_index < height_count // 2
+    turn_id = (time_index, jnp.where(low, 0, height_count - 1))
+    bent_id = (time_index, jnp.where(low, 4, height_count - 5))
+    bend_end_id = (time_index, jnp.where(low, 3, height_count - 4))
+    query_mate = (time_index, jnp.where(bent, turn_id[1], far_mate[1]))
+
     x, z_hi = height_index // 4, lax.rem(height_index // 2, 2)
     y, z_lo = time_index // Z_LO, lax.rem(time_index, Z_LO)
-    source_hi = jnp.where(z_lo < Z_LO // 2, z_hi, 1 - z_hi)
-    active = core == 1 - source_hi
+    active = core == 1 - z_hi
     hub = active & (z_lo == 0)
     root = time_index == 0
     face = hub & root
@@ -68,14 +76,8 @@
         (time_index, (lax.rem(x + d, XS) * 2 + z_hi) * 2 + core) for d in range(1, XS)
     ]
 
-    def at_z(z):
-        return (y * Z_LO + lax.rem(z, Z_LO), (x * 2 + z // Z_LO) * 2 + core)
-
-    leaves = [
-        at_z(lax.rem(z_hi * Z_LO + d + 2 * Z_LO, 2 * Z_LO))
-        for d in (-4, 3, -3, 2, -2, 1, -1)
-    ]
-    my_hub = at_z(source_hi * Z_LO)
+    leaves = [(y * Z_LO + d, height_index) for d in range(Z_LO - 1, 0, -1)]
+    my_hub = (y * Z_LO, height_index)
 
     barrier = pltpu.get_barrier_semaphore()
     pl.semaphore_signal(barrier, inc=1, device_id=core_mate, device_id_type=MESH)
@@ -85,7 +87,13 @@
         def _():
             pl.semaphore_signal(barrier, inc=1, device_id=mate_id, device_id_type=MESH)
 
-    for exists, group in ((active, y_peers + x_peers), (hub, leaves), (leaf, [my_hub])):
+    for exists, group in (
+        (active, y_peers + x_peers),
+        (hub, leaves),
+        (leaf, [my_hub]),
+        (bent | bend_end, [turn_id]),
+        (turn, [bent_id, bend_end_id]),
+    ):
 
         @pl.when(exists)
         def _():
@@ -94,6 +102,7 @@
 
     peers = 1 + sum(exists.astype(jnp.int32) for exists in (has_down, has_up, has_far, leaf))
     peers = peers + 6 * active.astype(jnp.int32) + 7 * hub.astype(jnp.int32)
+    peers = peers + (bent | bend_end).astype(jnp.int32) + 2 * turn.astype(jnp.int32)
     pl.semaphore_wait(barrier, peers)
 
     def remote(index, src, dst, device, arrival=None):
@@ -127,7 +136,11 @@
 
     def send_query(group):
         cut = columns(group)
-        return remote(QUERY + group, queries.at[:, cut], far_queries.at[:, cut], far_mate)
+        return remote(QUERY + group, queries.at[:, cut], far_queries.at[:, cut], query_mate)
+
+    def turn_query(group):
+        here = far_queries.at[:, columns(group)]
+        return remote(QUERY + group, here, here, bend_end_id)
 
     def send_part(group):
         cut = columns(group)
@@ -213,6 +226,12 @@
         join_core().wait()
         for kv in range(2):
             picked[kv] = partial[kv] + mate_partial[kv]
+
+    @pl.when(turn)
+    def _():
+        for group in range(GROUPS):
+            turn_query(group).wait_recv()
+            turn_query(group).start()
 
     @pl.when(face)
     def _():
@@ -426,6 +445,11 @@
         for kv in range(2):
             send_down(kv).wait_send()
             pass_first(kv).wait_send()
+
+    @pl.when(turn)
+    def _():
+        for group in range(GROUPS):
+            turn_query(group).wait_send()
 
     @pl.when(face)
     def _():
@@ -498,7 +522,7 @@
             pltpu.SemaphoreType.DMA((3,)),
         ],
         compiler_params=pltpu.CompilerParams(
-            collective_id=0, has_side_effects=True, vmem_limit_bytes=48 * 1024 * 1024
+            collective_id=0, has_side_effects=True, vmem_limit_bytes=60 * 1024 * 1024
         ),
         name="attention",
     )(queries.reshape(tokens, feat), keys_values.reshape(2, tokens, feat), ids)

time: 251 us -> 238 us (0.948)
  the two profiles are of different devices: /device:TPU:162 before, /device:TPU:11 now
where the time goes in v3:
time: 238 us
  Pallas kernels  234 us (98%)
  local copies, waits for them, and re-layouts  3.76 us (2%)
    pallas_call x1, Pallas kernels, per_device(): pl.pallas_call(kernel, out_shape=jax.ShapeDtypeStruct((tokens, feat), bf1...  234 us

profile of v3, /device:TPU:11, one launch (start us, length us, event | category | flops | bytes accessed | tf_op | source)
XLA Modules:
  0.0 238.1 jit_solution(9873523331855056634)
XLA Ops:
  0.0 0.7 reshape.16
  0.7 0.1 broadcast_in_dim.7
  0.8 0.7 broadcast_in_dim.8.anchor_ids
  1.5 234.3 %attention.1 = bf16[192,2560]{1,0:T(8,128)(2,1)} custom-call(bf16[192,2560]{1,0:T(8,128)(2,1)} %bitcast.5, bf16[2,192,2560]{2,1,0:T(8,128)(2,1)} %bitcast.4, s32[128,128]{1,0:T(8,128)} %broadcast_in_dim.8.anchor_ids), custom_call_target="tpu_custom_call" | custom-call | tf_op jit(solution)/shard_map/attention/pallas_call | solution.py:492
  235.9 2.2 copy.5
  (1 shorter events, 0.0 us)

commit v4 on v3

--- a/solution.py
+++ b/solution.py
@@ -17,7 +17,8 @@
 CORE, UP, DOWN, PASS_UP, PASS_DOWN, QUERY = 0, 2, 4, 6, 8, 10
 PART = QUERY + GROUPS
 STAT = PART + GROUPS
-JOIN = STAT + GROUPS
+PAIRS = (GROUPS + 1) // 2
+JOIN = STAT + PAIRS
 SCATTER = JOIN + 2
 SPREAD = SCATTER + 4
 ALONG_Y = SPREAD + 8
@@ -146,8 +147,8 @@
         cut = columns(group)
         return remote(PART + group, sent_part.at[:, cut], far_part.at[:, cut], far_mate)
 
-    def send_stat(group):
-        return remote(STAT + group, sent_stat.at[group], far_stat.at[group], far_mate)
+    def send_stat(pair):
+        return remote(STAT + pair, sent_stat.at[pair], far_stat.at[pair], far_mate)
 
     def slot(index):
         return pl.ds(pl.multiple_of(index * SLOT, SLOT), SLOT)
@@ -343,7 +344,8 @@
         part = weighted(weights, own[1, around, cut]) / total
         sent_part[here, cut] = part.astype(sent_part.dtype)
         level = top + jnp.log(total) * LOG2E
-        stat_block[here, :] = jnp.where(lane == head, level, stat_block[here, :])
+        place = group % 2 * per_group + head
+        stat_block[here, :] = jnp.where(lane == place, level, stat_block[here, :])
 
     @pl.when(has_far)
     def _():
@@ -355,9 +357,10 @@
             def _(step):
                 far_block(group, step)
 
-            sent_stat[group] = jnp.transpose(stat_block[...])[0:8]
             send_part(group).start()
-            send_stat(group).start()
+            if group % 2 == 1 or group == GROUPS - 1:
+                sent_stat[group // 2] = jnp.transpose(stat_block[...])[0:8]
+                send_stat(group // 2).start()
 
     for kv in range(2):
         share(kv).wait_recv()
@@ -418,12 +421,14 @@
         @pl.when(has_far)
         def _():
             send_part(group).wait_recv()
-            send_stat(group).wait_recv()
-
-        stats = jnp.transpose(far_stat[group])
+            if group % 2 == 0:
+                send_stat(group // 2).wait_recv()
+
+        stats = jnp.transpose(far_stat[group // 2])
         for head in range(per_group):
             cut = pl.ds((group * per_group + head) * size, size)
-            far_level = stats[0:tokens, head : head + 1]
+            place = group % 2 * per_group + head
+            far_level = stats[0:tokens, place : place + 1]
             mine = own_level[:, cut]
             top = jnp.maximum(mine, far_level)
             mine = jnp.exp2(mine - top)
@@ -475,7 +480,8 @@
         for group in range(GROUPS):
             send_query(group).wait_send()
             send_part(group).wait_send()
-            send_stat(group).wait_send()
+        for pair in range(PAIRS):
+            send_stat(pair).wait_send()
 
 
 def per_device(tm_count, height_count, queries, keys_values, anchor_ids):
@@ -505,8 +511,8 @@
             pltpu.VMEM((tokens, feat), bf16),
             pltpu.VMEM((tokens, feat), bf16),
             pltpu.VMEM((tokens, feat), bf16),
-            pltpu.VMEM((GROUPS, 8, padded), f32),
-            pltpu.VMEM((GROUPS, 8, padded), f32),
+            pltpu.VMEM((PAIRS, 8, padded), f32),
+            pltpu.VMEM((PAIRS, 8, padded), f32),
             pltpu.VMEM((tokens, feat), f32),
             pltpu.VMEM((tokens, feat), f32),
             pltpu.VMEM((frames, band, 3 * band), f32),

time: 238 us -> 237 us (level)
  no operation moved by 1% of the time
where the time goes in v4:
time: 237 us
  Pallas kernels  233 us (98%)
  local copies, waits for them, and re-layouts  3.76 us (2%)
    pallas_call x1, Pallas kernels, per_device(): pl.pallas_call(kernel, out_shape=jax.ShapeDtypeStruct((tokens, feat), bf1...  233 us

profile of v4, /device:TPU:11, one launch (start us, length us, event | category | flops | bytes accessed | tf_op | source)
XLA Modules:
  0.0 236.8 jit_solution(3065839278643907245)
XLA Ops:
  0.0 0.7 reshape.16
  0.7 0.1 broadcast_in_dim.7
  0.8 0.7 broadcast_in_dim.8.anchor_ids
  1.5 233.0 %attention.1 = bf16[192,2560]{1,0:T(8,128)(2,1)} custom-call(bf16[192,2560]{1,0:T(8,128)(2,1)} %bitcast.5, bf16[2,192,2560]{2,1,0:T(8,128)(2,1)} %bitcast.4, s32[128,128]{1,0:T(8,128)} %broadcast_in_dim.8.anchor_ids), custom_call_target="tpu_custom_call" | custom-call | tf_op jit(solution)/shard_map/attention/pallas_call | solution.py:498
  234.5 2.2 copy.5
  (1 shorter events, 0.0 us)
